TPU v7x, 128 devices: a whole 4x4x4 slice. The times are simulated.
128 devices in a mesh: dp: 2 (over z_lo), expert: 64 (over y, z_hi, x, core).
Axes of the slice: x: 4, y: 4, z: 4 (z_hi: 2, z_lo: 2; z = z_hi * 2 + z_lo), core: 2. Of those that a mesh axis runs over, the one named last changes fastest.
Arguments:
- tokens: bfloat16 [16384, 2048], P(('dp', 'expert')), may hold values from -6 to 6
- out_grad: bfloat16 [16384, 2048], P(('dp', 'expert')), may hold values from -6 to 6
- expert_ids: int32 [16384, 4], P(('dp', 'expert')), may hold values from 0 to 63, all different within a row; in each aligned block of 128 rows (0 to 127, 128 to 255, ...) at most 12 rows name the same one
- gate_probs: float32 [16384, 4], P(('dp', 'expert')), may hold values from 0.05 to 0.6
- w_gate: bfloat16 [64, 2048, 768], P('expert'), may hold values from -0.125 to 0.125
- w_up: bfloat16 [64, 2048, 768], P('expert'), may hold values from -0.125 to 0.125
- w_down: bfloat16 [64, 768, 2048], P('expert'), may hold values from -0.21875 to 0.21875
Outputs:
- layer_output: bfloat16 [16384, 2048], P(('dp', 'expert'))
- input_grad: bfloat16 [16384, 2048], P(('dp', 'expert'))
- probs_grad: float32 [16384, 4], P(('dp', 'expert'))
- gate_grad: bfloat16 [64, 2048, 768], P('expert', 'dp')
- up_grad: bfloat16 [64, 2048, 768], P('expert', 'dp')
- down_grad: bfloat16 [64, 768, 2048], P('expert', None, 'dp')
Inputs may be any that keep to these rules, and one draw needn't show every extreme that they name: `expert_ids`: each row names 4 different experts; within the 128 rows of one device no expert is named by more than 12 rows.
All inputs are finite; a program needn't handle non-finite values.
Results may differ from a plain program's by a relative error of at most 0.0064.
Values may be sent and summed in bfloat16 or wider, within the bound.
A program may use at most 192 MiB of HBM per device.

v0:
```python
import jax
import jax.numpy as jnp
from jax import lax
from jax.sharding import PartitionSpec as P


def forward_expert(rows_in, gate_w, up_w, down_w):
    act_gate = jnp.dot(rows_in, gate_w, preferred_element_type=jnp.float32)
    act_up = jnp.dot(rows_in, up_w, preferred_element_type=jnp.float32)
    hidden = (jax.nn.silu(act_gate) * act_up).astype(jnp.bfloat16)
    out_rows = jnp.dot(hidden, down_w, preferred_element_type=jnp.float32).astype(jnp.bfloat16)
    return (act_gate, act_up, hidden, out_rows)


def backward_expert(grads_in, act_gate, act_up, gate_w, up_w, down_w):
    contract = (((1,), (1,)), ((), ()))
    hidden_grad = lax.dot_general(grads_in, down_w, contract, preferred_element_type=jnp.float32)
    sig = jax.nn.sigmoid(act_gate)
    pre_gate = (hidden_grad * act_up * sig * (1.0 + act_gate * (1.0 - sig))).astype(jnp.bfloat16)
    pre_up = (hidden_grad * act_gate * sig).astype(jnp.bfloat16)
    row_grad = (
        lax.dot_general(pre_gate, gate_w, contract, preferred_element_type=jnp.float32)
        + lax.dot_general(pre_up, up_w, contract, preferred_element_type=jnp.float32)
    ).astype(jnp.bfloat16)
    return (row_grad, jnp.concatenate([pre_gate, pre_up], 1))


def weight_terms(slot_rows, slot_grads, gate_up, hidden):
    contract = (((0,), (0,)), ((), ()))
    left = lax.dot_general(slot_rows, gate_up, contract, preferred_element_type=jnp.float32)
    right = lax.dot_general(slot_grads, hidden, contract, preferred_element_type=jnp.float32)
    return jnp.concatenate([left, right], 1)


def per_device(tokens, out_grad, expert_ids, gate_probs, w_gate, w_up, w_down):
    tok, topk = expert_ids.shape
    width = tokens.shape[1]
    inner = w_gate.shape[2]
    experts = lax.axis_size("expert")
    cap = 3 * tok * topk // (2 * experts)
    count = tok * topk
    flat_ids = expert_ids.reshape(count)
    onehot = (flat_ids[:, None] == jnp.arange(experts, dtype=jnp.int32)[None, :]).astype(jnp.int32)
    ranks = jnp.sum(jnp.cumsum(onehot, 0) * onehot, 1) - 1
    dest = flat_ids * cap + ranks
    hits = dest[:, None] == jnp.arange(experts * cap, dtype=jnp.int32)[None, :]
    filled = jnp.any(hits, 0)
    owner = jnp.sum(jnp.where(hits, jnp.arange(count, dtype=jnp.int32)[:, None], 0), 0)
    owner = jnp.where(filled, owner, count)
    zero_row = jnp.zeros((1, width), jnp.bfloat16)
    token_ext = jnp.concatenate([tokens, zero_row], 0)
    scaled = (gate_probs[:, :, None] * out_grad[:, None, :].astype(jnp.float32)).astype(
        jnp.bfloat16
    )
    scaled_ext = jnp.concatenate([scaled.reshape(count, width), zero_row], 0)
    send_tokens = jnp.take(token_ext, owner // topk, axis=0).reshape(experts, cap, width)
    send_scaled = jnp.take(scaled_ext, owner, axis=0).reshape(experts, cap, width)
    gate_w = w_gate[0]
    up_w = w_up[0]
    down_w = w_down[0]
    rows_in = lax.all_to_all(
        send_tokens, "expert", split_axis=0, concat_axis=0, tiled=True
    ).reshape(experts * cap, width)
    act_gate, act_up, hidden, out_rows = forward_expert(rows_in, gate_w, up_w, down_w)
    back_out = lax.all_to_all(
        out_rows.reshape(experts, cap, width), "expert", split_axis=0, concat_axis=0, tiled=True
    )
    grads_in = lax.all_to_all(
        send_scaled, "expert", split_axis=0, concat_axis=0, tiled=True
    ).reshape(experts * cap, width)
    row_grad, gate_up = backward_expert(grads_in, act_gate, act_up, gate_w, up_w, down_w)
    back_grad = lax.all_to_all(
        row_grad.reshape(experts, cap, width), "expert", split_axis=0, concat_axis=0, tiled=True
    )
    picked = (
        jnp.take(back_out.reshape(experts * cap, width), dest, axis=0)
        .reshape(tok, topk, width)
        .astype(jnp.float32)
    )
    layer_output = jnp.sum(gate_probs[:, :, None] * picked, 1).astype(jnp.bfloat16)
    probs_grad = jnp.sum(picked * out_grad[:, None, :].astype(jnp.float32), 2)
    returned = jnp.take(back_grad.reshape(experts * cap, width), dest, axis=0).reshape(
        tok, topk, width
    )
    input_grad = jnp.sum(returned.astype(jnp.float32), 1).astype(jnp.bfloat16)
    total = lax.psum_scatter(
        weight_terms(rows_in, grads_in, gate_up, hidden), "dp", scatter_dimension=0, tiled=True
    )
    gate_grad = total[:, :inner].astype(jnp.bfloat16)[None]
    up_grad = total[:, inner : 2 * inner].astype(jnp.bfloat16)[None]
    down_grad = total[:, 2 * inner :].T.astype(jnp.bfloat16)[None]
    return (layer_output, input_grad, probs_grad, gate_grad, up_grad, down_grad)


def solution(mesh):
    return jax.shard_map(
        per_device,
        mesh=mesh,
        in_specs=(
            P(("dp", "expert"), None),
            P(("dp", "expert"), None),
            P(("dp", "expert"), None),
            P(("dp", "expert"), None),
            P("expert", None, None),
            P("expert", None, None),
            P("expert", None, None),
        ),
        out_specs=(
            P(("dp", "expert"), None),
            P(("dp", "expert"), None),
            P(("dp", "expert"), None),
            P("expert", "dp", None),
            P("expert", "dp", None),
            P("expert", None, "dp"),
        ),
        check_vma=False,
    )
```

profile of v0, /device:TPU:1, one launch (start us, length us, event | category | flops | bytes accessed | tf_op | source)
XLA Modules:
  0.0 504.6 jit_solution(16867993525091051855)
XLA Ops:
  12.6 8.2 %gather_fusion = bf16[768,2048]{1,0:T(8,128)(2,1)} fusion(bf16[129,2048]{1,0:T(8,128)(2,1)} %concatenate.12, s32[1024]{0:T(1024)S(1)} %get-tuple-element.40), kind=kCustom, calls=%fused_computation.2 | custom fusion | bytes 6294528 | tf_op jit(solution)/shard_map/jit(_take)/gather | solution.py:56
  20.9 6.1 %gather.16 = bf16[64,12,2048]{2,1,0:T(8,128)(2,1)} reshape(bf16[768,2048]{1,0:T(8,128)(2,1)} %gather_fusion) | data formatting | bytes 6291456 | tf_op jit(solution)/shard_map/jit(_take)/gather | solution.py:56
  31.6 12.6 %all-to-all-start = ((bf16[64,12,2048]{2,1,0:T(8,128)(2,1)}), bf16[64,12,2048]{2,1,0:T(8,128)(2,1)}, u32[]{:S(2)}, u32[]{:S(2)}) async-start(bf16[64,12,2048]{2,1,0:T(8,128)(2,1)} %broadcast_select_fusion.1), calls=%async_computation | async-start | bytes 8388608 | tf_op jit(solution)/shard_map/all_to_all | solution.py:61
  57.9 9.0 %gather_fusion.1 = bf16[768,2048]{1,0:T(8,128)(2,1)} fusion(bf16[513,2048]{1,0:T(8,128)(2,1)} %concatenate.13, s32[1024]{0:T(1024)S(1)} %get-tuple-element.39), kind=kCustom, calls=%fused_computation.3 | custom fusion | bytes 6294528 | tf_op jit(solution)/shard_map/jit(_take)/gather | solution.py:57
  66.9 6.1 %gather.18 = bf16[64,12,2048]{2,1,0:T(8,128)(2,1)} reshape(bf16[768,2048]{1,0:T(8,128)(2,1)} %gather_fusion.1) | data formatting | bytes 6291456 | tf_op jit(solution)/shard_map/jit(_take)/gather | solution.py:57
  77.6 19.9 %all-to-all-done = bf16[64,12,2048]{2,1,0:T(8,128)(2,1)} async-done(((bf16[64,12,2048]{2,1,0:T(8,128)(2,1)}), bf16[64,12,2048]{2,1,0:T(8,128)(2,1)}, u32[]{:S(2)}, u32[]{:S(2)}) %all-to-all-start) | async-done | bytes 3145760 | tf_op jit(solution)/shard_map/all_to_all | solution.py:61
  103.5 6.2 %reshape.191 = bf16[768,2048]{1,0:T(8,128)(2,1)} reshape(bf16[64,12,2048]{2,1,0:T(8,128)(2,1)} %all-to-all-done) | data formatting | bytes 6291456 | tf_op jit(solution)/shard_map/reshape | solution.py:63
  109.7 7.0 %fusion.4 = f32[768,768]{0,1:T(8,128)} fusion(bf16[768,2048]{1,0:T(8,128)(2,1)} %reshape.191, bf16[1,2048,768]{2,1,0:T(8,128)(2,1)} %param.14), kind=kOutput, calls=%fused_computation.16 | convolution fusion | flops 2415919104 | bytes 8650752 | tf_op jit(solution)/shard_map/dot_general | solution.py:9
  120.9 35.6 %all-to-all-done.2 = bf16[64,12,2048]{2,1,0:T(8,128)(2,1)} async-done(((bf16[64,12,2048]{2,1,0:T(8,128)(2,1)}), bf16[64,12,2048]{2,1,0:T(8,128)(2,1)}, u32[]{:S(2)}, u32[]{:S(2)}) %all-to-all-start.2) | async-done | bytes 3145760 | tf_op jit(solution)/shard_map/all_to_all | solution.py:68
  156.5 6.2 %reshape.194 = bf16[768,2048]{1,0:T(8,128)(2,1)} reshape(bf16[64,12,2048]{2,1,0:T(8,128)(2,1)} %all-to-all-done.2) | data formatting | bytes 6291456 | tf_op jit(solution)/shard_map/reshape | solution.py:70
  162.7 6.9 %multiply_convert_fusion.1 = (bf16[768,768]{0,1:T(8,128)(2,1)S(1)}, bf16[768,768]{0,1:T(8,128)(2,1)S(1)}, bf16[768,768]{0,1:T(8,128)(2,1)S(1)}) fusion(f32[768,768]{0,1:T(8,128)} %fusion.8, f32[768,768]{0,1:T(8,128)} %fusion.4, bf16[768,2048]{1,0:T(8,128)(2,1)} %reshape.194, bf16[1,768,2048]{2,1,0:T(8,128)(2,1)S(1)} %copy-done), kind=kOutput, calls=%fused_computation.26 | convolution fusion | flops 2425356288 | bytes 14548992 | tf_op jit(solution)/shard_map/dot_general | solution.py:17
  177.9 7.0 %pad_maximum_fusion = f32[2048,2304]{0,1:T(8,128)} fusion(f32[2048,768]{0,1:T(8,128)S(1)} %fusion.23, f32[2048,1536]{0,1:T(8,128)S(1)} %fusion.10), kind=kLoop, calls=%fused_computation.4 | loop fusion | flops 4718592 | bytes 37748736 | tf_op jit(solution)/shard_map/concatenate | solution.py:32
  190.2 6.2 %reshape.192 = bf16[64,12,2048]{2,1,0:T(8,128)(2,1)} reshape(bf16[768,2048]{1,0:T(8,128)(2,1)} %convolution_convert_fusion) | data formatting | bytes 6291456 | tf_op jit(solution)/shard_map/reshape | solution.py:66
  196.4 5.9 %all-to-all-start.1 = ((bf16[64,12,2048]{2,1,0:T(8,128)(2,1)}), bf16[64,12,2048]{2,1,0:T(8,128)(2,1)}, u32[]{:S(2)}, u32[]{:S(2)}) async-start(bf16[64,12,2048]{2,1,0:T(8,128)(2,1)} %reshape.192), calls=%async_computation.1 | async-start | bytes 8388608 | tf_op jit(solution)/shard_map/all_to_all | solution.py:65
  211.6 6.1 %reshape.195 = bf16[64,12,2048]{2,1,0:T(8,128)(2,1)} reshape(bf16[768,2048]{1,0:T(8,128)(2,1)} %add_convert_fusion) | data formatting | bytes 6291456 | tf_op jit(solution)/shard_map/reshape | solution.py:73
  217.6 37.9 %all-to-all-done.1 = bf16[64,12,2048]{2,1,0:T(8,128)(2,1)} async-done(((bf16[64,12,2048]{2,1,0:T(8,128)(2,1)}), bf16[64,12,2048]{2,1,0:T(8,128)(2,1)}, u32[]{:S(2)}, u32[]{:S(2)}) %all-to-all-start.1) | async-done | bytes 3145760 | tf_op jit(solution)/shard_map/all_to_all | solution.py:65
  255.5 6.2 %all-to-all-start.3 = ((bf16[64,12,2048]{2,1,0:T(8,128)(2,1)}), bf16[64,12,2048]{2,1,0:T(8,128)(2,1)}, u32[]{:S(2)}, u32[]{:S(2)}) async-start(bf16[64,12,2048]{2,1,0:T(8,128)(2,1)} %reshape.195), calls=%async_computation.3 | async-start | bytes 8388608 | tf_op jit(solution)/shard_map/all_to_all | solution.py:72
  261.8 6.2 %reshape.193 = bf16[768,2048]{1,0:T(8,128)(2,1)} reshape(bf16[64,12,2048]{2,1,0:T(8,128)(2,1)} %all-to-all-done.1) | data formatting | bytes 6291456 | tf_op jit(solution)/shard_map/reshape | solution.py:76
  268.0 7.5 %gather_fusion.2 = bf16[512,2048]{1,0:T(8,128)(2,1)} fusion(bf16[768,2048]{1,0:T(8,128)(2,1)} %reshape.193, s32[1024]{0:T(1024)S(1)} %pad_clamp_fusion.1), kind=kCustom, calls=%fused_computation.clone | custom fusion | bytes 4196352 | tf_op jit(solution)/shard_map/jit(_take)/gather | solution.py:76
  279.9 35.2 %all-to-all-done.3 = bf16[64,12,2048]{2,1,0:T(8,128)(2,1)} async-done(((bf16[64,12,2048]{2,1,0:T(8,128)(2,1)}), bf16[64,12,2048]{2,1,0:T(8,128)(2,1)}, u32[]{:S(2)}, u32[]{:S(2)}) %all-to-all-start.3) | async-done | bytes 3145760 | tf_op jit(solution)/shard_map/all_to_all | solution.py:72
  315.1 6.2 %reshape.196 = bf16[768,2048]{1,0:T(8,128)(2,1)} reshape(bf16[64,12,2048]{2,1,0:T(8,128)(2,1)} %all-to-all-done.3) | data formatting | bytes 6291456 | tf_op jit(solution)/shard_map/reshape | solution.py:82
  321.3 7.6 %gather_fusion.3 = bf16[512,2048]{1,0:T(8,128)(2,1)} fusion(bf16[768,2048]{1,0:T(8,128)(2,1)} %reshape.196, s32[1024]{0:T(1024)S(1)} %pad_clamp_fusion.1), kind=kCustom, calls=%fused_computation.1.clone | custom fusion | bytes 4196352 | tf_op jit(solution)/shard_map/jit(_take)/gather | solution.py:82
  348.9 6.2 %multiply_reduce_fusion.1 = bf16[128,2048]{1,0:T(8,128)(2,1)} fusion(f32[128,4,2048]{2,1,0:T(4,128)} %reshape.198, f32[128,4]{1,0:T(8,128)S(1)} %copy.24), kind=kLoop, calls=%fused_computation.8 | loop fusion | flops 1835008 | bytes 4720640 | tf_op jit(solution)/shard_map/reduce_sum | solution.py:80
  355.1 130.4 %reduce-scatter.2.cloned.1.call-done = f32[1024,2304]{0,1:T(8,128)} async-done(((f32[2048,2304]{0,1:T(8,128)}), f32[1024,2304]{0,1:T(8,128)}) %reduce-scatter.2.cloned.1.call-update) | async-done | bytes 9437200 | tf_op jit(solution)/shard_map/reduce_scatter | solution.py:86
  (70 shorter events, 97.6 us)
Async XLA Ops:
  7.2 155.5 %copy-start = (bf16[1,768,2048]{2,1,0:T(8,128)(2,1)S(1)}, bf16[1,768,2048]{2,1,0:T(8,128)(2,1)}, u32[]{:S(2)}) copy-start(bf16[1,768,2048]{2,1,0:T(8,128)(2,1)} %param.15) | copy-start | bytes 9437188
  31.5 12.6 %copy-start.4 = (f32[128,4]{0,1:T(4,128)S(1)}, f32[128,4]{0,1:T(4,128)}, u32[]{:S(2)}) copy-start(f32[128,4]{0,1:T(4,128)} %param.12) | copy-start | bytes 6148
  31.6 65.9 %all-to-all-start = ((bf16[64,12,2048]{2,1,0:T(8,128)(2,1)}), bf16[64,12,2048]{2,1,0:T(8,128)(2,1)}, u32[]{:S(2)}, u32[]{:S(2)}) async-start(bf16[64,12,2048]{2,1,0:T(8,128)(2,1)} %broadcast_select_fusion.1), calls=%async_computation | async-start | bytes 8388608 | tf_op jit(solution)/shard_map/all_to_all | solution.py:61
  97.5 59.0 %all-to-all-start.2 = ((bf16[64,12,2048]{2,1,0:T(8,128)(2,1)}), bf16[64,12,2048]{2,1,0:T(8,128)(2,1)}, u32[]{:S(2)}, u32[]{:S(2)}) async-start(bf16[64,12,2048]{2,1,0:T(8,128)(2,1)} %broadcast_select_fusion), calls=%async_computation.2 | async-start | bytes 8388608 | tf_op jit(solution)/shard_map/all_to_all | solution.py:68
  103.2 382.4 %reduce-scatter.2.cloned.1.call-start = ((), (), s32[]{:S(2)}) async-start(), calls=%async_computation.5 | async-start | bytes 28311552 | tf_op jit(solution)/shard_map/reduce_scatter | solution.py:86
  109.7 7.0 %copy-start.1 = (bf16[768,2048]{1,0:T(8,128)(2,1)S(1)}, bf16[768,2048]{1,0:T(8,128)(2,1)}, u32[]{:S(2)}) copy-start(bf16[768,2048]{1,0:T(8,128)(2,1)} %reshape.191) | copy-start | bytes 9437188
  109.7 7.0 %copy-start.5 = (bf16[1,2048,768]{2,1,0:T(8,128)(2,1)S(1)}, bf16[1,2048,768]{2,1,0:T(8,128)(2,1)}, u32[]{:S(2)}) copy-start(bf16[1,2048,768]{2,1,0:T(8,128)(2,1)} %param.13) | copy-start | bytes 9437188
  162.7 7.0 %copy-start.3 = (bf16[768,2048]{1,0:T(8,128)(2,1)S(1)}, bf16[768,2048]{1,0:T(8,128)(2,1)}, u32[]{:S(2)}) copy-start(bf16[768,2048]{1,0:T(8,128)(2,1)} %reshape.194) | copy-start | bytes 9437188
  169.6 2.7 copy-start.8
  169.6 2.7 copy-start.7
  169.6 2.7 copy-start.9
  169.6 3.1 copy-start.2
  196.4 59.1 %all-to-all-start.1 = ((bf16[64,12,2048]{2,1,0:T(8,128)(2,1)}), bf16[64,12,2048]{2,1,0:T(8,128)(2,1)}, u32[]{:S(2)}, u32[]{:S(2)}) async-start(bf16[64,12,2048]{2,1,0:T(8,128)(2,1)} %reshape.192), calls=%async_computation.1 | async-start | bytes 8388608 | tf_op jit(solution)/shard_map/all_to_all | solution.py:65
  202.3 5.1 %copy-start.6 = (bf16[1,2048,768]{2,1,0:T(8,128)(2,1)S(1)}, bf16[1,2048,768]{2,1,0:T(8,128)(2,1)}, u32[]{:S(2)}) copy-start(bf16[1,2048,768]{2,1,0:T(8,128)(2,1)} %param.14) | copy-start | bytes 9437188
  202.3 5.1 %copy-start.10 = (bf16[768,768]{0,1:T(8,128)(2,1)S(1)}, bf16[768,768]{0,1:T(8,128)(2,1)}, u32[]{:S(2)}) copy-start(bf16[768,768]{0,1:T(8,128)(2,1)} %copy-done.9) | copy-start | bytes 3538948
  255.5 59.6 %all-to-all-start.3 = ((bf16[64,12,2048]{2,1,0:T(8,128)(2,1)}), bf16[64,12,2048]{2,1,0:T(8,128)(2,1)}, u32[]{:S(2)}, u32[]{:S(2)}) async-start(bf16[64,12,2048]{2,1,0:T(8,128)(2,1)} %reshape.195), calls=%async_computation.3 | async-start | bytes 8388608 | tf_op jit(solution)/shard_map/all_to_all | solution.py:72
Sparse Core Ops, SparseCore 0:
  185.0 300.5 reduce-scatter.1
where the time goes:
time: 514 us; the launch traced here: 505 us
  waiting for transfers between devices  259 us (50%)
  local copies, waits for them, and re-layouts  114 us (22%)
  other arithmetic  45.3 us (9%)
  matrix products  40.4 us (8%)
  starting transfers between devices  30.7 us (6%)
  between operations  14.6 us (3%)
    reduce_scatter x1, waiting for transfers between devices, per_device(): lax.psum_scatter(weight_terms(rows_in, grads_in, gate_up, hidden), 'dp',...  130 us
    all_to_all x1, waiting for transfers between devices, per_device(): lax.all_to_all(out_rows.reshape(experts, cap, width), 'expert', split_axi...  37.9 us
    all_to_all x1, waiting for transfers between devices, per_device(): lax.all_to_all(send_scaled, 'expert', split_axis=0, concat_axis=0, tiled=...  35.6 us
    all_to_all x1, waiting for transfers between devices, per_device(): lax.all_to_all(row_grad.reshape(experts, cap, width), 'expert', split_axi...  35.2 us
    all_to_all x1, waiting for transfers between devices, per_device(): lax.all_to_all(send_tokens, 'expert', split_axis=0, concat_axis=0, tiled=...  19.9 us
    gather x2, local copies, waits for them, and re-layouts, per_device(): jnp.take(scaled_ext, owner, axis=0).reshape(experts, cap, width)  15 us
    gather x2, local copies, waits for them, and re-layouts, per_device(): jnp.take(token_ext, owner // topk, axis=0).reshape(experts, cap, width)  14.3 us
    all_to_all x1, starting transfers between devices, per_device(): lax.all_to_all(send_tokens, 'expert', split_axis=0, concat_axis=0, tiled=...  12.6 us
  transfers between devices with their start and end apart: 5, of which 5 were waited for; matrix products, arithmetic and copies ran while one was open for 27% of the time, Pallas kernels for 0%

commit v1 on v0

v1 whole, which is shorter than its diff:
```python
import functools

import jax
import jax.numpy as jnp
import numpy as np
from jax import lax
from jax.experimental import pallas as pl
from jax.experimental.pallas import tpu as pltpu
from jax.sharding import PartitionSpec as P

MESH = pl.DeviceIdType.MESH
BF = jnp.bfloat16
F32 = jnp.float32

CAP = 12
ROWS = 16
T0, T1, G0, G1, O0, O1, R0, R1 = range(8)
SEND = {T0: 0, T1: 1, G0: 2, G1: 0, O0: 1, O1: 2, R0: 0, R1: 1}


def dot(a, b):
    return jnp.dot(a, b, preferred_element_type=F32)


def dot_nt(a, b):
    return lax.dot_general(a, b, (((1,), (1,)), ((), ())), preferred_element_type=F32)


def dot_tn(a, b):
    return lax.dot_general(a, b, (((0,), (0,)), ((), ())), preferred_element_type=F32)


def kernel(
    ids_ref, probs_ref, tok_ref, grad_ref, triu_ref, umat_ref, vmat_ref, wg_hbm, wu_hbm, wd_hbm,
    lay_out, inp_out, prb_out, gate_out, up_out, down_out, mid,
    send, recv, wg, wu, wd, rows, grads, act, hidden, pre, wide,
    ztok, zgrad, zids, zprobs, zlay_s, zinp_s, zprb_s, zlay_r, zinp_r, zprb_r,
    lay_acc, prb_acc, dprows, dppre, dpdown, dsend,
    wsem, ssem, rsem, xs, xr,
):
    tok_n, D = tok_ref.shape
    FF = wg.shape[1]
    Q = D // 4
    HALF = D // 2
    NB = recv.shape[2] * recv.shape[3] * 2
    GR = NB * CAP
    CR = GR // 2

    d = lax.axis_index("dp")
    e = lax.axis_index("expert")
    c = e % 2
    x = (e // 2) % 4
    zh = (e // 8) % 2
    y = e // 16

    def at(dp, yy, zz, xx, cc):
        return (dp, ((yy * 2 + zz) * 4 + xx) * 2 + cc)

    def px(k, dc):
        return at(d, y, zh, (x + k) % 4, (c + dc) % 2)

    def py(k, dc):
        return at(d, (y + k) % 4, zh, x, (c + dc) % 2)

    pz = at(1 - d, y, 1 - zh, x, c)
    pdp = (1 - d, e)
    pcore = at(d, y, zh, x, 1 - c)

    barrier = pltpu.get_barrier_semaphore()
    peers = [px(k, dc) for k in (1, 2, 3) for dc in (0, 1)]
    peers += [py(k, dc) for k in (1, 2, 3) for dc in (0, 1)]
    peers += [pz, pdp, pcore]
    for p in peers:
        pl.semaphore_signal(barrier, inc=1, device_id=p, device_id_type=MESH)

    weights = [
        pltpu.make_async_copy(src, dst, wsem.at[i])
        for i, (src, dst) in enumerate(((wg_hbm, wg), (wu_hbm, wu), (wd_hbm, wd)))
    ]
    for cp in weights:
        cp.start()

    pl.semaphore_wait(barrier, len(peers))

    def remote(src, dst, ss, rs, to):
        cp = pltpu.make_async_remote_copy(
            src_ref=src, dst_ref=dst, send_sem=ss, recv_sem=rs, device_id=to, device_id_type=MESH
        )
        cp.start()
        return cp

    count = [0]
    extras = []

    def extra(src, dst, to):
        i = count[0]
        count[0] += 1
        cp = remote(src, dst, xs.at[i], xr.at[i], to)
        extras.append(cp)
        return cp

    z_ids = extra(ids_ref, zids, pz)
    z_probs = extra(probs_ref, zprobs, pz)
    z_tok = extra(tok_ref, ztok, pz)
    z_grad = extra(grad_ref, zgrad, pz)

    firsts, finals = {}, {}

    def first_legs(b):
        s = SEND[b]
        mids, ends = [], []
        n = 0
        for k in (1, 3, 2):
            for dc in (0, 1):
                to = px(k, 0) if dc == 0 else py(k, 1)
                mids.append(remote(
                    send.at[s, dc, k, pl.ds(1, 3)], mid.at[b, dc, k - 1],
                    ssem.at[b, n], rsem.at[b, n], to,
                ))
                n += 1
        for k in (1, 3, 2):
            for dc in (0, 1):
                to = px(k, 0) if dc == 0 else py(k, 1)
                ends.append(remote(
                    send.at[s, dc, k, 0], recv.at[b, dc, k, 0],
                    ssem.at[b, n], rsem.at[b, n], to,
                ))
                n += 1
                to = py(k, 0) if dc == 0 else px(k, 1)
                ends.append(remote(
                    send.at[s, dc, 0, k], recv.at[b, dc, 0, k],
                    ssem.at[b, n], rsem.at[b, n], to,
                ))
                n += 1
        ends.append(remote(
            send.at[s, 1, 0, 0], recv.at[b, 1, 0, 0], ssem.at[b, n], rsem.at[b, n], pcore,
        ))
        recv[b, 0, 0, 0] = send[s, 0, 0, 0]
        firsts[b] = (mids, ends)

    def second_legs(b):
        mids, ends = firsts[b]
        for cp in mids:
            cp.wait_recv()
        n = 19
        seconds = []
        for k in (1, 3, 2):
            for dc in (0, 1):
                to = py(k, 0) if dc == 0 else px(k, 0)
                seconds.append(remote(
                    mid.at[b, dc, pl.ds(0, 3), k - 1], recv.at[b, dc, pl.ds(1, 3), k],
                    ssem.at[b, n], rsem.at[b, n], to,
                ))
                n += 1
        finals[b] = ends + seconds

    def arrived(b):
        for cp in finals[b]:
            cp.wait_recv()

    sent = set()

    def sent_first(b):
        for cp in firsts[b][0] + firsts[b][1]:
            cp.wait_send()
        sent.add(b)

    def route(ids, probs, sign):
        b = lax.broadcasted_iota(jnp.int32, (NB, tok_n), 0)
        dc = b >> 4
        k1 = (b >> 2) & 3
        k2 = b & 3
        dx = jnp.where(dc == 0, k1, k2)
        dy = jnp.where(dc == 0, k2, k1)
        ee = ((((y + sign * dy) & 3) * 2 + zh) * 4 + ((x + sign * dx) & 3)) * 2 + ((c + dc) & 1)
        named = jnp.zeros((NB, tok_n), F32)
        prob = jnp.zeros((NB, tok_n), F32)
        for k in range(4):
            hit = ids[k : k + 1, :] == ee
            named = named + jnp.where(hit, 1.0, 0.0)
            prob = prob + jnp.where(hit, probs[k : k + 1, :], 0.0)
        rank = dot(named.astype(BF), triu_ref[...])
        pos = jnp.where(named > 0.0, rank, -100.0).astype(jnp.int32)
        return ee, pos, prob

    def slots(pos):
        shape = (NB, ROWS, tok_n)
        i = lax.broadcasted_iota(jnp.int32, shape, 1)
        at_pos = jnp.broadcast_to(pos[:, None, :], shape)
        main = at_pos == i
        ext = [at_pos == (i - CAP) * 3 + s for s in range(3)]
        return main, ext

    def flat(v):
        return v.reshape(NB * ROWS, tok_n)

    def ones(mask):
        return flat(jnp.where(mask, 1.0, 0.0)).astype(BF)

    def weighted(mask, prob):
        v = flat(jnp.where(mask, jnp.broadcast_to(prob[:, None, :], mask.shape), 0.0))
        hi = v.astype(BF)
        return hi, (v - hi.astype(F32)).astype(BF)

    def seg(s):
        return pl.ds(s * Q, Q)

    def pack_tokens(b, route_of, src):
        _, pos, _ = route_of
        main, ext = slots(pos)
        main = ones(main)
        for s in range(3):
            lhs = jnp.concatenate([main, ones(ext[s])], 1)
            rhs = jnp.concatenate([src[:, seg(s)], src[:, seg(3)]], 0)
            send[SEND[b], :, :, :, :, seg(s)] = dot(lhs, rhs).astype(BF).reshape(2, 4, 4, ROWS, Q)

    def pack_grads(b, route_of, src):
        _, pos, prob = route_of
        main, ext = slots(pos)
        main_hi, main_lo = weighted(main, prob)
        for s in range(3):
            ext_hi, ext_lo = weighted(ext[s], prob)
            lhs = jnp.concatenate([main_hi, ext_hi, main_lo, ext_lo], 1)
            rhs = jnp.concatenate([src[:, seg(s)], src[:, seg(3)]], 0)
            rhs = jnp.concatenate([rhs, rhs], 0)
            send[SEND[b], :, :, :, :, seg(s)] = dot(lhs, rhs).astype(BF).reshape(2, 4, 4, ROWS, Q)

    def unpack(b, dst, w):
        for dc in range(2):
            r = pl.ds(w * GR + dc * CR, CR)
            last = jnp.zeros((CR, Q), F32)
            for s in range(3):
                piece = recv[b, dc, :, :, :, seg(s)].reshape(16 * ROWS, Q)
                dst[r, seg(s)] = dot(umat_ref[0], piece).astype(BF)
                last = last + dot(umat_ref[s + 1], piece)
            dst[r, seg(3)] = last.astype(BF)

    def pack_rows(b):
        for dc in range(2):
            r = pl.ds(dc * CR, CR)
            for s in range(3):
                piece = dot(vmat_ref[0], wide[r, seg(s)]) + dot(vmat_ref[s + 1], wide[r, seg(3)])
                send[SEND[b], dc, :, :, :, seg(s)] = piece.astype(BF).reshape(4, 4, ROWS, Q)

    TF = 256

    def forward(w, b):
        r = pl.ds(w * GR, GR)

        @pl.loop(0, FF // TF)
        def _(n):
            col = pl.ds(pl.multiple_of(n * TF, TF), TF)
            ag = dot(rows[r, :], wg[:, col])
            au = dot(rows[r, :], wu[:, col])
            act[0, r, col] = ag
            act[1, r, col] = au
            hidden[r, col] = (ag * (1.0 / (1.0 + jnp.exp(-ag))) * au).astype(BF)

        @pl.loop(0, D // Q)
        def _(n):
            col = pl.ds(pl.multiple_of(n * Q, Q), Q)
            wide[:, col] = dot(hidden[r, :], wd[:, col]).astype(BF)

        pack_rows(b)

    def backward(w, b):
        r = pl.ds(w * GR, GR)

        @pl.loop(0, FF // TF)
        def _(n):
            col = pl.ds(pl.multiple_of(n * TF, TF), TF)
            hg = dot_nt(grads[r, :], wd[col, :])
            ag = act[0, r, col]
            s = 1.0 / (1.0 + jnp.exp(-ag))
            pre[0, r, col] = (hg * act[1, r, col] * s * (1.0 + ag * (1.0 - s))).astype(BF)
            pre[1, r, col] = (hg * (ag * s)).astype(BF)

        @pl.loop(0, D // TF)
        def _(n):
            col = pl.ds(pl.multiple_of(n * TF, TF), TF)
            total = dot_nt(pre[0, r, :], wg[col, :]) + dot_nt(pre[1, r, :], wu[col, :])
            wide[:, col] = total.astype(BF)

        pack_rows(b)

    def combine_out(b, route_of, ids, g_ref, lay, prb):
        ee, pos, prob = route_of
        main, ext = slots(pos)
        main_hi, main_lo = weighted(main, prob)
        main_m = flat(jnp.where(main, 1.0, 0.0))
        last = jnp.zeros((tok_n, Q), F32)
        inner = jnp.zeros((NB * ROWS, tok_n), F32)
        for s in range(3):
            ext_hi, ext_lo = weighted(ext[s], prob)
            piece = recv[b, :, :, :, :, seg(s)].reshape(NB * ROWS, Q)
            both = dot_tn(jnp.concatenate([main_hi, ext_hi], 1), piece)
            both = both + dot_tn(jnp.concatenate([main_lo, ext_lo], 1), piece)
            lay[:, seg(s)] = both[:tok_n].astype(lay.dtype)
            last = last + both[tok_n:]
            ext_m = flat(jnp.where(ext[s], 1.0, 0.0))
            inner = inner + dot_nt(piece, g_ref[:, seg(s)]) * main_m
            inner = inner + dot_nt(piece, g_ref[:, seg(3)]) * ext_m
        lay[:, seg(3)] = last.astype(lay.dtype)
        inner = jnp.sum(inner.reshape(NB, ROWS, tok_n), 1)
        for k in range(4):
            hit = ids[k : k + 1, :] == ee
            prb[k : k + 1, :] = jnp.sum(jnp.where(hit, inner, 0.0), 0, keepdims=True)
        prb[4:8, :] = jnp.zeros((4, tok_n), F32)

    def combine_grad(b, route_of, dst):
        _, pos, _ = route_of
        main, ext = slots(pos)
        main = ones(main)
        last = jnp.zeros((tok_n, Q), F32)
        for s in range(3):
            piece = recv[b, :, :, :, :, seg(s)].reshape(NB * ROWS, Q)
            both = dot_tn(jnp.concatenate([main, ones(ext[s])], 1), piece)
            dst[:, seg(s)] = both[:tok_n].astype(dst.dtype)
            last = last + both[tok_n:]
        dst[:, seg(3)] = last.astype(dst.dtype)

    mine = pl.multiple_of(d * HALF, HALF)
    other = pl.multiple_of((1 - d) * HALF, HALF)

    def dp_rows(w):
        r = pl.ds(w * GR, GR)
        return extra(rows.at[r, pl.ds(other, HALF)], dprows.at[r], pdp)

    def dp_pre(w):
        r = pl.ds(w * GR, GR)
        return [extra(pre.at[i, r], dppre.at[i, r], pdp) for i in range(2)]

    own_ids, own_probs = ids_ref[...], probs_ref[...]
    to_own = route(own_ids, own_probs, 1)
    pack_tokens(T0, to_own, tok_ref)
    first_legs(T0)
    pack_grads(G0, to_own, grad_ref)
    z_ids.wait_recv()
    z_probs.wait_recv()
    z_ids_v, z_probs_v = zids[...], zprobs[...]
    to_z = route(z_ids_v, z_probs_v, 1)
    z_tok.wait_recv()
    pack_tokens(T1, to_z, ztok)
    first_legs(T1)
    second_legs(T0)
    first_legs(G0)
    z_grad.wait_recv()
    sent_first(T0)
    pack_grads(G1, to_z, zgrad)
    second_legs(T1)
    first_legs(G1)

    for cp in weights:
        cp.wait()
    arrived(T0)
    unpack(T0, rows, 0)
    dp_in = [dp_rows(0)]
    sent_first(T1)
    forward(0, O0)
    second_legs(G0)
    first_legs(O0)
    arrived(T1)
    unpack(T1, rows, 1)
    dp_in.append(dp_rows(1))
    sent_first(G0)
    forward(1, O1)
    second_legs(G1)
    first_legs(O1)

    arrived(G0)
    unpack(G0, grads, 0)
    sent_first(G1)
    backward(0, R0)
    dp_in += dp_pre(0)
    second_legs(O0)
    first_legs(R0)
    arrived(G1)
    unpack(G1, grads, 1)
    sent_first(O0)
    backward(1, R1)
    dp_in += dp_pre(1)
    second_legs(O1)
    first_legs(R1)

    FB = 256

    @pl.loop(0, FF // FB)
    def _(n):
        col = pl.ds(pl.multiple_of(n * FB, FB), FB)
        dsend[col, :] = dot_tn(hidden[:, col], grads[:, pl.ds(other, HALF)]).astype(BF)

    dp_down = extra(dsend, dpdown, pdp)

    arrived(O0)
    own_back = route(own_ids, own_probs, -1)
    combine_out(O0, own_back, own_ids, grad_ref, lay_acc, prb_acc)
    second_legs(R0)
    arrived(O1)
    z_back = route(z_ids_v, z_probs_v, -1)
    combine_out(O1, z_back, z_ids_v, zgrad, zlay_s, zprb_s)
    z_lay = extra(zlay_s, zlay_r, pz)
    z_prb = extra(zprb_s, zprb_r, pz)
    second_legs(R1)

    for cp in dp_in:
        cp.wait_recv()

    @pl.loop(0, HALF // FB)
    def _(n):
        at_n = pl.multiple_of(n * FB, FB)
        own = rows[:, pl.ds(mine + at_n, FB)]
        theirs = dprows[:, pl.ds(at_n, FB)]
        for i, out in enumerate((gate_out, up_out)):
            total = dot_tn(own, pre[i]) + dot_tn(theirs, dppre[i])
            out[pl.ds(at_n, FB), :] = total.astype(BF)

    arrived(R1)
    combine_grad(R1, z_back, zinp_s)
    z_inp = extra(zinp_s, zinp_r, pz)
    z_lay.wait_recv()
    lay_out[...] = (lay_acc[...] + zlay_r[...].astype(F32)).astype(BF)
    z_prb.wait_recv()
    prb_out[...] = prb_acc[...] + zprb_r[...]
    arrived(R0)
    combine_grad(R0, own_back, lay_acc)

    dp_down.wait_recv()

    @pl.loop(0, FF // FB)
    def _(n):
        col = pl.ds(pl.multiple_of(n * FB, FB), FB)
        own = dot_tn(hidden[:, col], grads[:, pl.ds(mine, HALF)])
        down_out[col, :] = (own + dpdown[col, :].astype(F32)).astype(BF)

    z_inp.wait_recv()
    inp_out[...] = (lay_acc[...] + zinp_r[...].astype(F32)).astype(BF)

    for b in range(8):
        if b not in sent:
            sent_first(b)
        for cp in finals[b][len(firsts[b][1]) :]:
            cp.wait_send()
    for cp in extras:
        cp.wait_send()


def matrices():
    u = np.zeros((4, 16, CAP, 16, ROWS), np.float32)
    v = np.zeros((4, 16, ROWS, 16, CAP), np.float32)
    for k in range(16):
        m = ((4 - k // 4) % 4) * 4 + (4 - k % 4) % 4
        for i in range(CAP):
            u[0, k, i, k, i] = 1
            v[0, m, i, k, i] = 1
            u[1 + i % 3, k, i, k, CAP + i // 3] = 1
            v[1 + i % 3, m, CAP + i // 3, k, i] = 1
    u = u.reshape(4, 16 * CAP, 16 * ROWS)
    v = v.reshape(4, 16 * ROWS, 16 * CAP)
    return jnp.asarray(u, BF), jnp.asarray(v, BF)


def per_device(tokens, out_grad, expert_ids, gate_probs, w_gate, w_up, w_down):
    tok_n, D = tokens.shape
    topk = expert_ids.shape[1]
    FF = w_gate.shape[2]
    W = 3 * D // 4
    slots = 64 * CAP
    ids = jnp.concatenate([expert_ids.T, jnp.full((8 - topk, tok_n), -1, jnp.int32)], 0)
    probs = jnp.concatenate([gate_probs.T, jnp.zeros((8 - topk, tok_n), F32)], 0)
    triu = jnp.asarray(np.triu(np.ones((tok_n, tok_n), np.float32), 1), BF)
    u, v = matrices()
    vm = pl.BlockSpec(memory_space=pltpu.VMEM)
    hbm = pl.BlockSpec(memory_space=pl.ANY)
    sds = jax.ShapeDtypeStruct
    V = pltpu.VMEM
    out = pl.pallas_call(
        kernel,
        out_shape=(
            sds((tok_n, D), BF), sds((tok_n, D), BF), sds((8, tok_n), F32),
            sds((D // 2, FF), BF), sds((D // 2, FF), BF), sds((FF, D // 2), BF),
            sds((8, 2, 3, 3, ROWS, W), BF),
        ),
        in_specs=[vm] * 7 + [hbm] * 3,
        out_specs=(vm,) * 6 + (hbm,),
        scratch_shapes=[
            V((3, 2, 4, 4, ROWS, W), BF), V((8, 2, 4, 4, ROWS, W), BF),
            V((D, FF), BF), V((D, FF), BF), V((FF, D), BF),
            V((slots, D), BF), V((slots, D), BF),
            V((2, slots, FF), F32), V((slots, FF), BF), V((2, slots, FF), BF),
            V((slots // 2, D), BF),
            V((tok_n, D), BF), V((tok_n, D), BF), V((8, tok_n), jnp.int32), V((8, tok_n), F32),
            V((tok_n, D), BF), V((tok_n, D), BF), V((8, tok_n), F32),
            V((tok_n, D), BF), V((tok_n, D), BF), V((8, tok_n), F32),
            V((tok_n, D), F32), V((8, tok_n), F32),
            V((slots, D // 2), BF), V((2, slots, FF), BF), V((FF, D // 2), BF), V((FF, D // 2), BF),
            pltpu.SemaphoreType.DMA((3,)),
            pltpu.SemaphoreType.DMA((8, 25)), pltpu.SemaphoreType.DMA((8, 25)),
            pltpu.SemaphoreType.DMA((16,)), pltpu.SemaphoreType.DMA((16,)),
        ],
        compiler_params=pltpu.CompilerParams(
            collective_id=0, has_side_effects=True, vmem_limit_bytes=63 * 2**20
        ),
        cost_estimate=pl.CostEstimate(
            flops=18 * slots * D * FF, bytes_accessed=20 * 2**20, transcendentals=2 * slots * FF
        ),
        name="moe",
    )(ids, probs, tokens, out_grad, triu, u, v, w_gate[0], w_up[0], w_down[0])
    lay, inp, prb, gate, up, down = out[:6]
    return lay, inp, prb[:topk].T, gate[None], up[None], down[None]


def solution(mesh):
    return jax.shard_map(
        per_device,
        mesh=mesh,
        in_specs=(
            P(("dp", "expert"), None),
            P(("dp", "expert"), None),
            P(("dp", "expert"), None),
            P(("dp", "expert"), None),
            P("expert", None, None),
            P("expert", None, None),
            P("expert", None, None),
        ),
        out_specs=(
            P(("dp", "expert"), None),
            P(("dp", "expert"), None),
            P(("dp", "expert"), None),
            P("expert", "dp", None),
            P("expert", "dp", None),
            P("expert", None, "dp"),
        ),
        check_vma=False,
    )
```

time: 514 us -> 189 us (0.37); the launches traced: 505 us -> 186 us
  waiting for transfers between devices: 259 us -> 0 us
  Pallas kernels: 0 us -> 172 us
  local copies, waits for them, and re-layouts: 114 us -> 12.8 us
  other arithmetic: 45.3 us -> 0 us
  matrix products: 40.4 us -> 0 us
  starting transfers between devices: 30.7 us -> 0 us
  between operations: 14.6 us -> 0.65 us
    pallas_call x0 -> x1, Pallas kernels: none -> 172 us  [per_device(): pl.pallas_call(kernel, out_shape=(sds((tok_n, D), BF), sds((tok_n, D), BF...]
    reduce_scatter x1 -> x0, waiting for transfers between devices: 130 us -> none  [per_device(): lax.psum_scatter(weight_terms(rows_in, grads_in, gate_up, hidden), 'dp',...]
    all_to_all x4 -> x0, waiting for transfers between devices: 129 us -> none  [the longest x1 37.9 us: per_device(): lax.all_to_all(out_rows.reshape(experts, cap, width), 'expert', split_axi...]
    gather x6 -> x0, local copies, waits for them, and re-layouts: 44.5 us -> none  [the longest x2 15 us: per_device(): jnp.take(scaled_ext, owner, axis=0).reshape(experts, cap, width)]
    reshape x8 -> x0, local copies, waits for them, and re-layouts: 41.2 us -> none  [the longest x1 6.24 us: per_device(): back_out.reshape(experts * cap, width)]
    dot_general x8 -> x0, matrix products: 40.4 us -> none  [the longest x1 7.04 us: forward_expert(): act_up = jnp.dot(rows_in, up_w, preferred_element_type=jnp.float32)]
    all_to_all x4 -> x0, starting transfers between devices: 30.4 us -> none  [the longest x1 12.6 us: per_device(): lax.all_to_all(send_tokens, 'expert', split_axis=0, concat_axis=0, tiled=...]
    reduce_sum x5 -> x0, other arithmetic: 15.1 us -> none  [the longest x1 6.2 us: per_device(): jnp.sum(gate_probs[:, :, None] * picked, 1).astype(jnp.bfloat16)]
  transfers between devices with their start and end apart: 5 -> 0, of which waited for: 5 -> 0; matrix products, arithmetic and copies ran while one was open for 27% -> 0% of each run, Pallas kernels for 0% -> 0%
where the time goes in v1:
time: 189 us; the launch traced here: 186 us
  Pallas kernels  172 us (91%)
  local copies, waits for them, and re-layouts  12.8 us (7%)
    pallas_call x1, Pallas kernels, per_device(): pl.pallas_call(kernel, out_shape=(sds((tok_n, D), BF), sds((tok_n, D), BF...  172 us
    unnamed x11, local copies, waits for them, and re-layouts  8.86 us

profile of v1, /device:TPU:1, one launch (start us, length us, event | category | flops | bytes accessed | tf_op | source)
XLA Modules:
  0.0 185.7 jit_solution(4746759190605056564)
XLA Ops:
  0.6 1.3 concatenate.6.ids_ref
  1.9 1.3 concatenate.7.probs_ref
  3.2 172.2 %moe.1 = (bf16[128,2048]{1,0:T(8,128)(2,1)}, bf16[128,2048]{1,0:T(8,128)(2,1)}, f32[8,128]{1,0:T(8,128)}, bf16[1024,768]{1,0:T(8,128)(2,1)}, bf16[1024,768]{1,0:...) custom-call(s32[8,128]{1,0:T(8,128)} %concatenate.6.ids_ref, ...), custom_call_target="tpu_custom_call" | custom-call | flops 21743271936 | bytes 20971520 | tf_op jit(solution)/shard_map/moe/pallas_call | solution.py:476
  175.4 0.0 copy-start.2
  175.4 1.4 slice_bitcast_fusion
  176.8 1.9 %copy.21 = bf16[128,2048]{1,0:T(8,128)(2,1)} copy(bf16[128,2048]{1,0:T(8,128)(2,1)} %get-tuple-element.24) | data formatting | bytes 1048576
  178.7 1.9 %copy.22 = bf16[128,2048]{1,0:T(8,128)(2,1)} copy(bf16[128,2048]{1,0:T(8,128)(2,1)} %get-tuple-element.25) | data formatting | bytes 1048576
  180.6 0.0 copy-done.2
  180.6 0.0 copy-start.1
  180.6 1.1 copy.23
  181.7 0.8 copy-done.1
  182.6 0.0 copy-start
  182.6 1.1 copy.24
  183.7 0.8 copy-done
  184.5 1.1 copy.25
Async XLA Ops:
  175.4 5.1 %copy-start.2 = (bf16[1024,768]{1,0:T(8,128)(2,1)S(1)}, bf16[1024,768]{1,0:T(8,128)(2,1)}, u32[]{:S(2)}) copy-start(bf16[1024,768]{1,0:T(8,128)(2,1)} %get-tuple-element.15) | copy-start | bytes 4718596
  180.6 2.0 %copy-start.1 = (bf16[1024,768]{1,0:T(8,128)(2,1)S(1)}, bf16[1024,768]{1,0:T(8,128)(2,1)}, u32[]{:S(2)}) copy-start(bf16[1024,768]{1,0:T(8,128)(2,1)} %get-tuple-element.16) | copy-start | bytes 4718596
  182.6 2.0 %copy-start = (bf16[768,1024]{1,0:T(8,128)(2,1)S(1)}, bf16[768,1024]{1,0:T(8,128)(2,1)}, u32[]{:S(2)}) copy-start(bf16[768,1024]{1,0:T(8,128)(2,1)} %get-tuple-element.17) | copy-start | bytes 4718596

commit v2 on v1

--- a/solution.py
+++ b/solution.py
@@ -15,7 +15,7 @@
 CAP = 12
 ROWS = 16
 T0, T1, G0, G1, O0, O1, R0, R1 = range(8)
-SEND = {T0: 0, T1: 1, G0: 2, G1: 0, O0: 1, O1: 2, R0: 0, R1: 1}
+SEND = {T0: 0, G0: 1, T1: 2, G1: 3, O0: 0, R0: 1, O1: 2, R1: 3}
 
 
 def dot(a, b):
@@ -35,7 +35,7 @@
     lay_out, inp_out, prb_out, gate_out, up_out, down_out, mid,
     send, recv, wg, wu, wd, rows, grads, act, hidden, pre, wide,
     ztok, zgrad, zids, zprobs, zlay_s, zinp_s, zprb_s, zlay_r, zinp_r, zprb_r,
-    lay_acc, prb_acc, dprows, dppre, dpdown, dsend,
+    lay_acc, prb_acc, dprows, dppre, dpdown, gate_v, up_v, down_v,
     wsem, ssem, rsem, xs, xr,
 ):
     tok_n, D = tok_ref.shape
@@ -244,7 +244,7 @@
 
     TF = 256
 
-    def forward(w, b):
+    def forward(w):
         r = pl.ds(w * GR, GR)
 
         @pl.loop(0, FF // TF)
@@ -256,6 +256,9 @@
             act[1, r, col] = au
             hidden[r, col] = (ag * (1.0 / (1.0 + jnp.exp(-ag))) * au).astype(BF)
 
+    def forward_out(w, b):
+        r = pl.ds(w * GR, GR)
+
         @pl.loop(0, D // Q)
         def _(n):
             col = pl.ds(pl.multiple_of(n * Q, Q), Q)
@@ -263,7 +266,7 @@
 
         pack_rows(b)
 
-    def backward(w, b):
+    def backward(w):
         r = pl.ds(w * GR, GR)
 
         @pl.loop(0, FF // TF)
@@ -274,6 +277,9 @@
             s = 1.0 / (1.0 + jnp.exp(-ag))
             pre[0, r, col] = (hg * act[1, r, col] * s * (1.0 + ag * (1.0 - s))).astype(BF)
             pre[1, r, col] = (hg * (ag * s)).astype(BF)
+
+    def backward_rows(w, b):
+        r = pl.ds(w * GR, GR)
 
         @pl.loop(0, D // TF)
         def _(n):
@@ -305,7 +311,6 @@
         for k in range(4):
             hit = ids[k : k + 1, :] == ee
             prb[k : k + 1, :] = jnp.sum(jnp.where(hit, inner, 0.0), 0, keepdims=True)
-        prb[4:8, :] = jnp.zeros((4, tok_n), F32)
 
     def combine_grad(b, route_of, dst):
         _, pos, _ = route_of
@@ -330,90 +335,80 @@
         r = pl.ds(w * GR, GR)
         return [extra(pre.at[i, r], dppre.at[i, r], pdp) for i in range(2)]
 
+    FB = FF // 2
+
+    def down_part(n, half):
+        return dot_tn(hidden[:, pl.ds(n * FB, FB)], grads[:, pl.ds(half, HALF)])
+
     own_ids, own_probs = ids_ref[...], probs_ref[...]
     to_own = route(own_ids, own_probs, 1)
     pack_tokens(T0, to_own, tok_ref)
     first_legs(T0)
     pack_grads(G0, to_own, grad_ref)
+    second_legs(T0)
+    first_legs(G0)
     z_ids.wait_recv()
     z_probs.wait_recv()
     z_ids_v, z_probs_v = zids[...], zprobs[...]
     to_z = route(z_ids_v, z_probs_v, 1)
     z_tok.wait_recv()
     pack_tokens(T1, to_z, ztok)
-    first_legs(T1)
-    second_legs(T0)
-    first_legs(G0)
-    z_grad.wait_recv()
-    sent_first(T0)
-    pack_grads(G1, to_z, zgrad)
-    second_legs(T1)
-    first_legs(G1)
-
     for cp in weights:
         cp.wait()
     arrived(T0)
     unpack(T0, rows, 0)
     dp_in = [dp_rows(0)]
-    sent_first(T1)
-    forward(0, O0)
+    first_legs(T1)
+    forward(0)
     second_legs(G0)
+    sent_first(T0)
+    forward_out(0, O0)
+    z_grad.wait_recv()
+    pack_grads(G1, to_z, zgrad)
+    first_legs(G1)
+    second_legs(T1)
+    arrived(G0)
+    unpack(G0, grads, 0)
+    backward(0)
+    dp_in += dp_pre(0)
     first_legs(O0)
+    sent_first(G0)
+    backward_rows(0, R0)
+    second_legs(G1)
     arrived(T1)
     unpack(T1, rows, 1)
     dp_in.append(dp_rows(1))
-    sent_first(G0)
-    forward(1, O1)
-    second_legs(G1)
+    sent_first(T1)
+    forward(1)
+    forward_out(1, O1)
     first_legs(O1)
-
-    arrived(G0)
-    unpack(G0, grads, 0)
-    sent_first(G1)
-    backward(0, R0)
-    dp_in += dp_pre(0)
     second_legs(O0)
-    first_legs(R0)
     arrived(G1)
     unpack(G1, grads, 1)
-    sent_first(O0)
-    backward(1, R1)
+    backward(1)
     dp_in += dp_pre(1)
+    sent_first(G1)
+    backward_rows(1, R1)
+    first_legs(R1)
     second_legs(O1)
-    first_legs(R1)
-
-    FB = 256
-
-    @pl.loop(0, FF // FB)
-    def _(n):
-        col = pl.ds(pl.multiple_of(n * FB, FB), FB)
-        dsend[col, :] = dot_tn(hidden[:, col], grads[:, pl.ds(other, HALF)]).astype(BF)
-
-    dp_down = extra(dsend, dpdown, pdp)
-
-    arrived(O0)
+    for n in range(2):
+        wide[:, pl.ds(n * HALF, HALF)] = down_part(n, other).astype(BF)
+    dp_down = extra(wide, dpdown, pdp)
+    first_legs(R0)
+    for n in range(2):
+        own = down_part(n, mine)
+        act[n, pl.ds(0, FB), :] = own[:, :FF]
+        act[n, pl.ds(FB, FB), pl.ds(0, HALF - FF)] = own[:, FF:]
+    second_legs(R1)
     own_back = route(own_ids, own_probs, -1)
-    combine_out(O0, own_back, own_ids, grad_ref, lay_acc, prb_acc)
-    second_legs(R0)
+    z_back = route(z_ids_v, z_probs_v, -1)
     arrived(O1)
-    z_back = route(z_ids_v, z_probs_v, -1)
     combine_out(O1, z_back, z_ids_v, zgrad, zlay_s, zprb_s)
     z_lay = extra(zlay_s, zlay_r, pz)
     z_prb = extra(zprb_s, zprb_r, pz)
-    second_legs(R1)
-
-    for cp in dp_in:
-        cp.wait_recv()
-
-    @pl.loop(0, HALF // FB)
-    def _(n):
-        at_n = pl.multiple_of(n * FB, FB)
-        own = rows[:, pl.ds(mine + at_n, FB)]
-        theirs = dprows[:, pl.ds(at_n, FB)]
-        for i, out in enumerate((gate_out, up_out)):
-            total = dot_tn(own, pre[i]) + dot_tn(theirs, dppre[i])
-            out[pl.ds(at_n, FB), :] = total.astype(BF)
-
+    arrived(O0)
+    combine_out(O0, own_back, own_ids, grad_ref, lay_acc, prb_acc)
+    second_legs(R0)
     arrived(R1)
     combine_grad(R1, z_back, zinp_s)
     z_inp = extra(zinp_s, zinp_r, pz)
@@ -421,19 +416,41 @@
     lay_out[...] = (lay_acc[...] + zlay_r[...].astype(F32)).astype(BF)
     z_prb.wait_recv()
     prb_out[...] = prb_acc[...] + zprb_r[...]
+
+    for cp in dp_in:
+        cp.wait_recv()
+
+    TG = 256
+
+    @pl.loop(0, HALF // TG)
+    def _(n):
+        at_n = pl.multiple_of(n * TG, TG)
+        own = rows[:, pl.ds(mine + at_n, TG)]
+        theirs = dprows[:, pl.ds(at_n, TG)]
+        for i, out in enumerate((gate_v, up_v)):
+            total = dot_tn(own, pre[i]) + dot_tn(theirs, dppre[i])
+            out[pl.ds(at_n, TG), :] = total.astype(BF)
+
+    stores = [pltpu.make_async_copy(gate_v, gate_out, wsem.at[0])]
+    stores.append(pltpu.make_async_copy(up_v, up_out, wsem.at[1]))
+    for cp in stores:
+        cp.start()
+
     arrived(R0)
     combine_grad(R0, own_back, lay_acc)
-
-    dp_down.wait_recv()
-
-    @pl.loop(0, FF // FB)
-    def _(n):
-        col = pl.ds(pl.multiple_of(n * FB, FB), FB)
-        own = dot_tn(hidden[:, col], grads[:, pl.ds(mine, HALF)])
-        down_out[col, :] = (own + dpdown[col, :].astype(F32)).astype(BF)
-
     z_inp.wait_recv()
     inp_out[...] = (lay_acc[...] + zinp_r[...].astype(F32)).astype(BF)
+
+    dp_down.wait_recv()
+    for n in range(2):
+        theirs = dpdown[:, pl.ds(n * HALF, HALF)].astype(F32)
+        r = pl.ds(n * FB, FB)
+        down_v[r, pl.ds(0, FF)] = (act[n, pl.ds(0, FB), :] + theirs[:, :FF]).astype(BF)
+        own = act[n, pl.ds(FB, FB), pl.ds(0, HALF - FF)]
+        down_v[r, pl.ds(FF, HALF - FF)] = (own + theirs[:, FF:]).astype(BF)
+    cp = pltpu.make_async_copy(down_v, down_out, wsem.at[2])
+    cp.start()
+    stores.append(cp)
 
     for b in range(8):
         if b not in sent:
@@ -442,6 +459,30 @@
             cp.wait_send()
     for cp in extras:
         cp.wait_send()
+    for cp in stores:
+        cp.wait()
+
+
+PARTS = 2
+
+
+def hand_over(*refs):
+    srcs, dsts, held, sem = refs[:6], refs[6:12], refs[12:18], refs[18]
+    loads, stores = [], []
+    for i in range(6):
+        parts = PARTS if srcs[i].shape[0] % (16 * PARTS) == 0 else 1
+        n = srcs[i].shape[0] // parts
+        for j in range(parts):
+            r = pl.ds(j * n, n)
+            loads.append(pltpu.make_async_copy(srcs[i].at[r], held[i].at[r], sem.at[0, i, j]))
+            stores.append(pltpu.make_async_copy(held[i].at[r], dsts[i].at[r], sem.at[1, i, j]))
+    for cp in loads:
+        cp.start()
+    for load, store in zip(loads, stores):
+        load.wait()
+        store.start()
+    for cp in stores:
+        cp.wait()
 
 
 def matrices():
@@ -465,8 +506,7 @@
     FF = w_gate.shape[2]
     W = 3 * D // 4
     slots = 64 * CAP
-    ids = jnp.concatenate([expert_ids.T, jnp.full((8 - topk, tok_n), -1, jnp.int32)], 0)
-    probs = jnp.concatenate([gate_probs.T, jnp.zeros((8 - topk, tok_n), F32)], 0)
+    ids, probs = expert_ids.T, gate_probs.T
     triu = jnp.asarray(np.triu(np.ones((tok_n, tok_n), np.float32), 1), BF)
     u, v = matrices()
     vm = pl.BlockSpec(memory_space=pltpu.VMEM)
@@ -476,23 +516,24 @@
     out = pl.pallas_call(
         kernel,
         out_shape=(
-            sds((tok_n, D), BF), sds((tok_n, D), BF), sds((8, tok_n), F32),
+            sds((tok_n, D), BF), sds((tok_n, D), BF), sds((topk, tok_n), F32),
             sds((D // 2, FF), BF), sds((D // 2, FF), BF), sds((FF, D // 2), BF),
             sds((8, 2, 3, 3, ROWS, W), BF),
         ),
         in_specs=[vm] * 7 + [hbm] * 3,
-        out_specs=(vm,) * 6 + (hbm,),
+        out_specs=(vm,) * 3 + (hbm,) * 4,
         scratch_shapes=[
-            V((3, 2, 4, 4, ROWS, W), BF), V((8, 2, 4, 4, ROWS, W), BF),
+            V((4, 2, 4, 4, ROWS, W), BF), V((8, 2, 4, 4, ROWS, W), BF),
             V((D, FF), BF), V((D, FF), BF), V((FF, D), BF),
             V((slots, D), BF), V((slots, D), BF),
             V((2, slots, FF), F32), V((slots, FF), BF), V((2, slots, FF), BF),
             V((slots // 2, D), BF),
-            V((tok_n, D), BF), V((tok_n, D), BF), V((8, tok_n), jnp.int32), V((8, tok_n), F32),
-            V((tok_n, D), BF), V((tok_n, D), BF), V((8, tok_n), F32),
-            V((tok_n, D), BF), V((tok_n, D), BF), V((8, tok_n), F32),
-            V((tok_n, D), F32), V((8, tok_n), F32),
-            V((slots, D // 2), BF), V((2, slots, FF), BF), V((FF, D // 2), BF), V((FF, D // 2), BF),
+            V((tok_n, D), BF), V((tok_n, D), BF), V((topk, tok_n), jnp.int32), V((topk, tok_n), F32),
+            V((tok_n, D), BF), V((tok_n, D), BF), V((topk, tok_n), F32),
+            V((tok_n, D), BF), V((tok_n, D), BF), V((topk, tok_n), F32),
+            V((tok_n, D), F32), V((topk, tok_n), F32),
+            V((slots, D // 2), BF), V((2, slots, FF), BF), V((slots // 2, D), BF),
+            V((D // 2, FF), BF), V((D // 2, FF), BF), V((FF, D // 2), BF),
             pltpu.SemaphoreType.DMA((3,)),
             pltpu.SemaphoreType.DMA((8, 25)), pltpu.SemaphoreType.DMA((8, 25)),
             pltpu.SemaphoreType.DMA((16,)), pltpu.SemaphoreType.DMA((16,)),
@@ -505,8 +546,15 @@
         ),
         name="moe",
     )(ids, probs, tokens, out_grad, triu, u, v, w_gate[0], w_up[0], w_down[0])
-    lay, inp, prb, gate, up, down = out[:6]
-    return lay, inp, prb[:topk].T, gate[None], up[None], down[None]
+    lay, inp, prb, gate, up, down = pl.pallas_call(
+        hand_over,
+        out_shape=[sds(o.shape, o.dtype) for o in out[:6]],
+        in_specs=[hbm] * 6,
+        out_specs=[hbm] * 6,
+        scratch_shapes=[V(o.shape, o.dtype) for o in out[:6]] + [pltpu.SemaphoreType.DMA((2, 6, PARTS))],
+        name="hand_over",
+    )(*out[:6])
+    return lay, inp, prb.T, gate[None], up[None], down[None]
 
 
 def solution(mesh):

time: 189 us -> 173 us (0.915); the launches traced: 186 us -> 172 us
  local copies, waits for them, and re-layouts: 12.8 us -> 0 us
    unnamed x11 -> x0, local copies, waits for them, and re-layouts: 8.86 us -> none
    pallas_call x1, Pallas kernels: 172 us -> 166 us  [per_device(): pl.pallas_call(kernel, out_shape=(sds((tok_n, D), BF), sds((tok_n, D), BF...]
    pallas_call x0 -> x1, Pallas kernels: none -> 5.06 us  [per_device(): pl.pallas_call(hand_over, out_shape=[sds(o.shape, o.dtype) for o in out[:...]
    concatenate x2 -> x0, local copies, waits for them, and re-layouts: 2.56 us -> none  [the longest x1 1.28 us: per_device(): jnp.concatenate([expert_ids.T, jnp.full((8 - topk, tok_n), -1, jnp.int32)...]
where the time goes in v2:
time: 173 us; the launch traced here: 172 us
  Pallas kernels  171 us (99%)
    pallas_call x1, Pallas kernels, per_device(): pl.pallas_call(kernel, out_shape=(sds((tok_n, D), BF), sds((tok_n, D), BF...  166 us
    pallas_call x1, Pallas kernels, per_device(): pl.pallas_call(hand_over, out_shape=[sds(o.shape, o.dtype) for o in out[:...  5.06 us

profile of v2, /device:TPU:1, one launch (start us, length us, event | category | flops | bytes accessed | tf_op | source)
XLA Modules:
  0.0 172.2 jit_solution(12746849740988683952)
XLA Ops:
  0.6 166.4 %moe.1 = (bf16[128,2048]{1,0:T(8,128)(2,1)}, bf16[128,2048]{1,0:T(8,128)(2,1)}, f32[4,128]{1,0:T(4,128)}, bf16[1024,768]{1,0:T(8,128)(2,1)}, bf16[1024,768]{1,0:...) custom-call(s32[4,128]{1,0:T(4,128)} %bitcast.15, f32[4,128]{1,0:T(4,128)} %bitcast.16, ...), custom_call_target="tpu_custom_call" | custom-call | flops 21743271936 | bytes 20971520 | tf_op jit(solution)/shard_map/moe/pallas_call | solution.py:516
  167.0 5.1 %hand_over.1 = (bf16[128,2048]{1,0:T(8,128)(2,1)}, bf16[128,2048]{1,0:T(8,128)(2,1)}, f32[4,128]{1,0:T(4,128)}, bf16[1024,768]{1,0:T(8,128)(2,1)}, bf16[1024,768]{1,0:T(8,128)(2,1)}, /*index=5*/bf16[768,1024]{1,0:T(8,128)(2,1)}) custom-call(bf16[128,2048]{1,0:T(8,128)(2,1)} %get-tuple-element.18.refs_0_, bf16[128,2048]{1,0:T(8,128)(2,1)} %get-tuple-element.19.refs_1_, ...), custom_call_target="tpu_custom_call" | custom-call | tf_op jit(solution)/shard_map/hand_over/pallas_call | solution.py:549

commit v3 on v2

--- a/solution.py
+++ b/solution.py
@@ -15,7 +15,7 @@
 CAP = 12
 ROWS = 16
 T0, T1, G0, G1, O0, O1, R0, R1 = range(8)
-SEND = {T0: 0, G0: 1, T1: 2, G1: 3, O0: 0, R0: 1, O1: 2, R1: 3}
+SEND = {T0: 0, T1: 1, G0: 2, G1: 3, O0: 0, O1: 1, R0: 2, R1: 3}
 
 
 def dot(a, b):
@@ -35,7 +35,7 @@
     lay_out, inp_out, prb_out, gate_out, up_out, down_out, mid,
     send, recv, wg, wu, wd, rows, grads, act, hidden, pre, wide,
     ztok, zgrad, zids, zprobs, zlay_s, zinp_s, zprb_s, zlay_r, zinp_r, zprb_r,
-    lay_acc, prb_acc, dprows, dppre, dpdown, gate_v, up_v, down_v,
+    lay_acc, prb_acc, dprows, dppre, dpdown,
     wsem, ssem, rsem, xs, xr,
 ):
     tok_n, D = tok_ref.shape
@@ -80,8 +80,6 @@
     for cp in weights:
         cp.start()
 
-    pl.semaphore_wait(barrier, len(peers))
-
     def remote(src, dst, ss, rs, to):
         cp = pltpu.make_async_remote_copy(
             src_ref=src, dst_ref=dst, send_sem=ss, recv_sem=rs, device_id=to, device_id_type=MESH
@@ -98,11 +96,6 @@
         cp = remote(src, dst, xs.at[i], xr.at[i], to)
         extras.append(cp)
         return cp
-
-    z_ids = extra(ids_ref, zids, pz)
-    z_probs = extra(probs_ref, zprobs, pz)
-    z_tok = extra(tok_ref, ztok, pz)
-    z_grad = extra(grad_ref, zgrad, pz)
 
     firsts, finals = {}, {}
 
@@ -312,14 +305,16 @@
             hit = ids[k : k + 1, :] == ee
             prb[k : k + 1, :] = jnp.sum(jnp.where(hit, inner, 0.0), 0, keepdims=True)
 
-    def combine_grad(b, route_of, dst):
-        _, pos, _ = route_of
-        main, ext = slots(pos)
+    def sum_matrices(route_of):
+        main, ext = slots(route_of[1])
         main = ones(main)
+        return [jnp.concatenate([main, ones(ext[s])], 1) for s in range(3)]
+
+    def combine_grad(b, sums, dst):
         last = jnp.zeros((tok_n, Q), F32)
         for s in range(3):
             piece = recv[b, :, :, :, :, seg(s)].reshape(NB * ROWS, Q)
-            both = dot_tn(jnp.concatenate([main, ones(ext[s])], 1), piece)
+            both = dot_tn(sums[s], piece)
             dst[:, seg(s)] = both[:tok_n].astype(dst.dtype)
             last = last + both[tok_n:]
         dst[:, seg(3)] = last.astype(dst.dtype)
@@ -343,44 +338,49 @@
     own_ids, own_probs = ids_ref[...], probs_ref[...]
     to_own = route(own_ids, own_probs, 1)
     pack_tokens(T0, to_own, tok_ref)
+    pl.semaphore_wait(barrier, len(peers))
+    z_ids = extra(ids_ref, zids, pz)
+    z_probs = extra(probs_ref, zprobs, pz)
+    z_tok = extra(tok_ref, ztok, pz)
+    z_grad = extra(grad_ref, zgrad, pz)
     first_legs(T0)
     pack_grads(G0, to_own, grad_ref)
-    second_legs(T0)
-    first_legs(G0)
     z_ids.wait_recv()
     z_probs.wait_recv()
     z_ids_v, z_probs_v = zids[...], zprobs[...]
     to_z = route(z_ids_v, z_probs_v, 1)
+    second_legs(T0)
     z_tok.wait_recv()
     pack_tokens(T1, to_z, ztok)
+    first_legs(T1)
     for cp in weights:
         cp.wait()
     arrived(T0)
     unpack(T0, rows, 0)
     dp_in = [dp_rows(0)]
-    first_legs(T1)
+    first_legs(G0)
+    second_legs(T1)
     forward(0)
-    second_legs(G0)
     sent_first(T0)
     forward_out(0, O0)
     z_grad.wait_recv()
     pack_grads(G1, to_z, zgrad)
+    second_legs(G0)
     first_legs(G1)
-    second_legs(T1)
+    arrived(T1)
+    unpack(T1, rows, 1)
+    dp_in.append(dp_rows(1))
+    forward(1)
+    sent_first(T1)
+    forward_out(1, O1)
+    second_legs(G1)
+    first_legs(O0)
     arrived(G0)
     unpack(G0, grads, 0)
     backward(0)
     dp_in += dp_pre(0)
-    first_legs(O0)
     sent_first(G0)
     backward_rows(0, R0)
-    second_legs(G1)
-    arrived(T1)
-    unpack(T1, rows, 1)
-    dp_in.append(dp_rows(1))
-    sent_first(T1)
-    forward(1)
-    forward_out(1, O1)
     first_legs(O1)
     second_legs(O0)
     arrived(G1)
@@ -409,8 +409,9 @@
     arrived(O0)
     combine_out(O0, own_back, own_ids, grad_ref, lay_acc, prb_acc)
     second_legs(R0)
+    z_sums = sum_matrices(z_back)
     arrived(R1)
-    combine_grad(R1, z_back, zinp_s)
+    combine_grad(R1, z_sums, zinp_s)
     z_inp = extra(zinp_s, zinp_r, pz)
     z_lay.wait_recv()
     lay_out[...] = (lay_acc[...] + zlay_r[...].astype(F32)).astype(BF)
@@ -427,17 +428,13 @@
         at_n = pl.multiple_of(n * TG, TG)
         own = rows[:, pl.ds(mine + at_n, TG)]
         theirs = dprows[:, pl.ds(at_n, TG)]
-        for i, out in enumerate((gate_v, up_v)):
+        for i, out in enumerate((gate_out, up_out)):
             total = dot_tn(own, pre[i]) + dot_tn(theirs, dppre[i])
             out[pl.ds(at_n, TG), :] = total.astype(BF)
 
-    stores = [pltpu.make_async_copy(gate_v, gate_out, wsem.at[0])]
-    stores.append(pltpu.make_async_copy(up_v, up_out, wsem.at[1]))
-    for cp in stores:
-        cp.start()
-
+    own_sums = sum_matrices(own_back)
     arrived(R0)
-    combine_grad(R0, own_back, lay_acc)
+    combine_grad(R0, own_sums, lay_acc)
     z_inp.wait_recv()
     inp_out[...] = (lay_acc[...] + zinp_r[...].astype(F32)).astype(BF)
 
@@ -445,13 +442,9 @@
     for n in range(2):
         theirs = dpdown[:, pl.ds(n * HALF, HALF)].astype(F32)
         r = pl.ds(n * FB, FB)
-        down_v[r, pl.ds(0, FF)] = (act[n, pl.ds(0, FB), :] + theirs[:, :FF]).astype(BF)
+        down_out[r, pl.ds(0, FF)] = (act[n, pl.ds(0, FB), :] + theirs[:, :FF]).astype(BF)
         own = act[n, pl.ds(FB, FB), pl.ds(0, HALF - FF)]
-        down_v[r, pl.ds(FF, HALF - FF)] = (own + theirs[:, FF:]).astype(BF)
-    cp = pltpu.make_async_copy(down_v, down_out, wsem.at[2])
-    cp.start()
-    stores.append(cp)
-
+        down_out[r, pl.ds(FF, HALF - FF)] = (own + theirs[:, FF:]).astype(BF)
     for b in range(8):
         if b not in sent:
             sent_first(b)
@@ -459,29 +452,14 @@
             cp.wait_send()
     for cp in extras:
         cp.wait_send()
-    for cp in stores:
-        cp.wait()
-
-
-PARTS = 2
 
 
 def hand_over(*refs):
-    srcs, dsts, held, sem = refs[:6], refs[6:12], refs[12:18], refs[18]
-    loads, stores = [], []
-    for i in range(6):
-        parts = PARTS if srcs[i].shape[0] % (16 * PARTS) == 0 else 1
-        n = srcs[i].shape[0] // parts
-        for j in range(parts):
-            r = pl.ds(j * n, n)
-            loads.append(pltpu.make_async_copy(srcs[i].at[r], held[i].at[r], sem.at[0, i, j]))
-            stores.append(pltpu.make_async_copy(held[i].at[r], dsts[i].at[r], sem.at[1, i, j]))
-    for cp in loads:
+    sem = refs[12]
+    copies = [pltpu.make_async_copy(refs[i], refs[6 + i], sem.at[i]) for i in range(6)]
+    for cp in copies:
         cp.start()
-    for load, store in zip(loads, stores):
-        load.wait()
-        store.start()
-    for cp in stores:
+    for cp in copies:
         cp.wait()
 
 
@@ -516,12 +494,12 @@
     out = pl.pallas_call(
         kernel,
         out_shape=(
-            sds((tok_n, D), BF), sds((tok_n, D), BF), sds((topk, tok_n), F32),
-            sds((D // 2, FF), BF), sds((D // 2, FF), BF), sds((FF, D // 2), BF),
+            V((tok_n, D), BF), V((tok_n, D), BF), V((topk, tok_n), F32),
+            V((D // 2, FF), BF), V((D // 2, FF), BF), V((FF, D // 2), BF),
             sds((8, 2, 3, 3, ROWS, W), BF),
         ),
         in_specs=[vm] * 7 + [hbm] * 3,
-        out_specs=(vm,) * 3 + (hbm,) * 4,
+        out_specs=(vm,) * 6 + (hbm,),
         scratch_shapes=[
             V((4, 2, 4, 4, ROWS, W), BF), V((8, 2, 4, 4, ROWS, W), BF),
             V((D, FF), BF), V((D, FF), BF), V((FF, D), BF),
@@ -533,13 +511,12 @@
             V((tok_n, D), BF), V((tok_n, D), BF), V((topk, tok_n), F32),
             V((tok_n, D), F32), V((topk, tok_n), F32),
             V((slots, D // 2), BF), V((2, slots, FF), BF), V((slots // 2, D), BF),
-            V((D // 2, FF), BF), V((D // 2, FF), BF), V((FF, D // 2), BF),
             pltpu.SemaphoreType.DMA((3,)),
             pltpu.SemaphoreType.DMA((8, 25)), pltpu.SemaphoreType.DMA((8, 25)),
             pltpu.SemaphoreType.DMA((16,)), pltpu.SemaphoreType.DMA((16,)),
         ],
         compiler_params=pltpu.CompilerParams(
-            collective_id=0, has_side_effects=True, vmem_limit_bytes=63 * 2**20
+            collective_id=0, has_side_effects=True, vmem_limit_bytes=57 * 2**20
         ),
         cost_estimate=pl.CostEstimate(
             flops=18 * slots * D * FF, bytes_accessed=20 * 2**20, transcendentals=2 * slots * FF
@@ -549,11 +526,12 @@
     lay, inp, prb, gate, up, down = pl.pallas_call(
         hand_over,
         out_shape=[sds(o.shape, o.dtype) for o in out[:6]],
-        in_specs=[hbm] * 6,
+        in_specs=[vm] * 6,
         out_specs=[hbm] * 6,
-        scratch_shapes=[V(o.shape, o.dtype) for o in out[:6]] + [pltpu.SemaphoreType.DMA((2, 6, PARTS))],
+        scratch_shapes=[pltpu.SemaphoreType.DMA((6,))],
+        compiler_params=pltpu.CompilerParams(vmem_limit_bytes=2**20),
         name="hand_over",
-    )(*out[:6])
+    )(*[pltpu.with_memory_space_constraint(o, pltpu.VMEM) for o in out[:6]])
     return lay, inp, prb.T, gate[None], up[None], down[None]
 
 

time: 173 us -> 166 us (0.960)
  Pallas kernels: 171 us -> 165 us
    pallas_call x1, Pallas kernels: 166 us -> 162 us  [per_device(): pl.pallas_call(kernel, out_shape=(V((tok_n, D), BF), V((tok_n, D), BF), V...]
    pallas_call x1, Pallas kernels: 5.06 us -> 2.58 us  [per_device(): pl.pallas_call(hand_over, out_shape=[sds(o.shape, o.dtype) for o in out[:...]
where the time goes in v3:
time: 166 us
  Pallas kernels  165 us (99%)
    pallas_call x1, Pallas kernels, per_device(): pl.pallas_call(kernel, out_shape=(V((tok_n, D), BF), V((tok_n, D), BF), V...  162 us

profile of v3, /device:TPU:1, one launch (start us, length us, event | category | flops | bytes accessed | tf_op | source)
XLA Modules:
  0.0 165.6 jit_solution(968456468586908911)
XLA Ops:
  0.6 162.2 %moe.1 = (bf16[128,2048]{1,0:T(8,128)(2,1)S(1)}, bf16[128,2048]{1,0:T(8,128)(2,1)S(1)}, f32[4,128]{1,0:T(4,128)S(1)}, bf16[1024,768]{1,0:T(8,128)(2,1)S(1)}, bf1...) custom-call(s32[4,128]{1,0:T(4,128)} %bitcast.15, ...), custom_call_target="tpu_custom_call" | custom-call | flops 21743271936 | bytes 20971520 | tf_op jit(solution)/shard_map/moe/pallas_call | solution.py:494
  162.8 2.6 %hand_over.1 = (bf16[128,2048]{1,0:T(8,128)(2,1)}, bf16[128,2048]{1,0:T(8,128)(2,1)}, f32[4,128]{1,0:T(4,128)}, bf16[1024,768]{1,0:T(8,128)(2,1)}, bf16[1024,768]{1,0:T(8,128)(2,1)}, /*index=5*/bf16[768,1024]{1,0:T(8,128)(2,1)}) custom-call(bf16[128,2048]{1,0:T(8,128)(2,1)S(1)} %get-tuple-element.18.refs_0_, ...), custom_call_target="tpu_custom_call" | custom-call | tf_op jit(solution)/shard_map/hand_over/pallas_call | solution.py:526

commit v4 on v3

--- a/solution.py
+++ b/solution.py
@@ -218,15 +218,21 @@
             rhs = jnp.concatenate([rhs, rhs], 0)
             send[SEND[b], :, :, :, :, seg(s)] = dot(lhs, rhs).astype(BF).reshape(2, 4, 4, ROWS, Q)
 
-    def unpack(b, dst, w):
+    def unpack(b, put, w):
         for dc in range(2):
             r = pl.ds(w * GR + dc * CR, CR)
             last = jnp.zeros((CR, Q), F32)
             for s in range(3):
                 piece = recv[b, dc, :, :, :, seg(s)].reshape(16 * ROWS, Q)
-                dst[r, seg(s)] = dot(umat_ref[0], piece).astype(BF)
+                put(r, s, dot(umat_ref[0], piece).astype(BF))
                 last = last + dot(umat_ref[s + 1], piece)
-            dst[r, seg(3)] = last.astype(BF)
+            put(r, 3, last.astype(BF))
+
+    def put_rows(r, s, value):
+        rows[s // 2, r, pl.ds(s % 2 * Q, Q)] = value
+
+    def put_grads(r, s, value):
+        grads[r, seg(s)] = value
 
     def pack_rows(b):
         for dc in range(2):
@@ -243,8 +249,9 @@
         @pl.loop(0, FF // TF)
         def _(n):
             col = pl.ds(pl.multiple_of(n * TF, TF), TF)
-            ag = dot(rows[r, :], wg[:, col])
-            au = dot(rows[r, :], wu[:, col])
+            lo, hi = pl.ds(0, HALF), pl.ds(HALF, HALF)
+            ag = dot(rows[0, r, :], wg[lo, col]) + dot(rows[1, r, :], wg[hi, col])
+            au = dot(rows[0, r, :], wu[lo, col]) + dot(rows[1, r, :], wu[hi, col])
             act[0, r, col] = ag
             act[1, r, col] = au
             hidden[r, col] = (ag * (1.0 / (1.0 + jnp.exp(-ag))) * au).astype(BF)
@@ -324,7 +331,7 @@
 
     def dp_rows(w):
         r = pl.ds(w * GR, GR)
-        return extra(rows.at[r, pl.ds(other, HALF)], dprows.at[r], pdp)
+        return extra(rows.at[1 - d, r], dprows.at[r], pdp)
 
     def dp_pre(w):
         r = pl.ds(w * GR, GR)
@@ -342,7 +349,6 @@
     z_ids = extra(ids_ref, zids, pz)
     z_probs = extra(probs_ref, zprobs, pz)
     z_tok = extra(tok_ref, ztok, pz)
-    z_grad = extra(grad_ref, zgrad, pz)
     first_legs(T0)
     pack_grads(G0, to_own, grad_ref)
     z_ids.wait_recv()
@@ -351,15 +357,16 @@
     to_z = route(z_ids_v, z_probs_v, 1)
     second_legs(T0)
     z_tok.wait_recv()
+    z_grad = extra(grad_ref, zgrad, pz)
     pack_tokens(T1, to_z, ztok)
     first_legs(T1)
     for cp in weights:
         cp.wait()
     arrived(T0)
-    unpack(T0, rows, 0)
+    unpack(T0, put_rows, 0)
     dp_in = [dp_rows(0)]
+    second_legs(T1)
     first_legs(G0)
-    second_legs(T1)
     forward(0)
     sent_first(T0)
     forward_out(0, O0)
@@ -368,32 +375,32 @@
     second_legs(G0)
     first_legs(G1)
     arrived(T1)
-    unpack(T1, rows, 1)
+    unpack(T1, put_rows, 1)
     dp_in.append(dp_rows(1))
     forward(1)
     sent_first(T1)
     forward_out(1, O1)
+    arrived(G0)
+    unpack(G0, put_grads, 0)
+    backward(0)
+    dp_in += dp_pre(0)
     second_legs(G1)
     first_legs(O0)
-    arrived(G0)
-    unpack(G0, grads, 0)
-    backward(0)
-    dp_in += dp_pre(0)
     sent_first(G0)
     backward_rows(0, R0)
     first_legs(O1)
-    second_legs(O0)
     arrived(G1)
-    unpack(G1, grads, 1)
+    unpack(G1, put_grads, 1)
     backward(1)
     dp_in += dp_pre(1)
+    second_legs(O0)
     sent_first(G1)
     backward_rows(1, R1)
     first_legs(R1)
-    second_legs(O1)
     for n in range(2):
         wide[:, pl.ds(n * HALF, HALF)] = down_part(n, other).astype(BF)
     dp_down = extra(wide, dpdown, pdp)
+    second_legs(O1)
     first_legs(R0)
     for n in range(2):
         own = down_part(n, mine)
@@ -426,7 +433,7 @@
     @pl.loop(0, HALF // TG)
     def _(n):
         at_n = pl.multiple_of(n * TG, TG)
-        own = rows[:, pl.ds(mine + at_n, TG)]
+        own = rows[d, :, pl.ds(at_n, TG)]
         theirs = dprows[:, pl.ds(at_n, TG)]
         for i, out in enumerate((gate_out, up_out)):
             total = dot_tn(own, pre[i]) + dot_tn(theirs, dppre[i])
@@ -503,7 +510,7 @@
         scratch_shapes=[
             V((4, 2, 4, 4, ROWS, W), BF), V((8, 2, 4, 4, ROWS, W), BF),
             V((D, FF), BF), V((D, FF), BF), V((FF, D), BF),
-            V((slots, D), BF), V((slots, D), BF),
+            V((2, slots, D // 2), BF), V((slots, D), BF),
             V((2, slots, FF), F32), V((slots, FF), BF), V((2, slots, FF), BF),
             V((slots // 2, D), BF),
             V((tok_n, D), BF), V((tok_n, D), BF), V((topk, tok_n), jnp.int32), V((topk, tok_n), F32),

time: 166 us -> 163 us (0.982)
  Pallas kernels: 165 us -> 162 us
    pallas_call x1, Pallas kernels: 162 us -> 159 us  [per_device(): pl.pallas_call(kernel, out_shape=(V((tok_n, D), BF), V((tok_n, D), BF), V...]
where the time goes in v4:
time: 163 us
  Pallas kernels  162 us (99%)
    pallas_call x1, Pallas kernels, per_device(): pl.pallas_call(kernel, out_shape=(V((tok_n, D), BF), V((tok_n, D), BF), V...  159 us

profile of v4, /device:TPU:1, one launch (start us, length us, event | category | flops | bytes accessed | tf_op | source)
XLA Modules:
  0.0 162.9 jit_solution(7854917349292960409)
XLA Ops:
  0.6 159.5 %moe.1 = (bf16[128,2048]{1,0:T(8,128)(2,1)S(1)}, bf16[128,2048]{1,0:T(8,128)(2,1)S(1)}, f32[4,128]{1,0:T(4,128)S(1)}, bf16[1024,768]{1,0:T(8,128)(2,1)S(1)}, bf1...) custom-call(s32[4,128]{1,0:T(4,128)} %bitcast.15, ...), custom_call_target="tpu_custom_call" | custom-call | flops 21743271936 | bytes 20971520 | tf_op jit(solution)/shard_map/moe/pallas_call | solution.py:501
  160.1 2.6 %hand_over.1 = (bf16[128,2048]{1,0:T(8,128)(2,1)}, bf16[128,2048]{1,0:T(8,128)(2,1)}, f32[4,128]{1,0:T(4,128)}, bf16[1024,768]{1,0:T(8,128)(2,1)}, bf16[1024,768]{1,0:T(8,128)(2,1)}, /*index=5*/bf16[768,1024]{1,0:T(8,128)(2,1)}) custom-call(bf16[128,2048]{1,0:T(8,128)(2,1)S(1)} %get-tuple-element.18.refs_0_, ...), custom_call_target="tpu_custom_call" | custom-call | tf_op jit(solution)/shard_map/hand_over/pallas_call | solution.py:533

commit v5 on v4

--- a/solution.py
+++ b/solution.py
@@ -103,7 +103,7 @@
         s = SEND[b]
         mids, ends = [], []
         n = 0
-        for k in (1, 3, 2):
+        for k in (2, 1, 3):
             for dc in (0, 1):
                 to = px(k, 0) if dc == 0 else py(k, 1)
                 mids.append(remote(
@@ -111,7 +111,7 @@
                     ssem.at[b, n], rsem.at[b, n], to,
                 ))
                 n += 1
-        for k in (1, 3, 2):
+        for k in (2, 1, 3):
             for dc in (0, 1):
                 to = px(k, 0) if dc == 0 else py(k, 1)
                 ends.append(remote(
@@ -137,7 +137,7 @@
             cp.wait_recv()
         n = 19
         seconds = []
-        for k in (1, 3, 2):
+        for k in (2, 1, 3):
             for dc in (0, 1):
                 to = py(k, 0) if dc == 0 else px(k, 0)
                 seconds.append(remote(
@@ -218,8 +218,8 @@
             rhs = jnp.concatenate([rhs, rhs], 0)
             send[SEND[b], :, :, :, :, seg(s)] = dot(lhs, rhs).astype(BF).reshape(2, 4, 4, ROWS, Q)
 
-    def unpack(b, put, w):
-        for dc in range(2):
+    def unpack(b, put, w, classes=(0, 1)):
+        for dc in classes:
             r = pl.ds(w * GR + dc * CR, CR)
             last = jnp.zeros((CR, Q), F32)
             for s in range(3):
@@ -266,9 +266,7 @@
 
         pack_rows(b)
 
-    def backward(w):
-        r = pl.ds(w * GR, GR)
-
+    def backward(r):
         @pl.loop(0, FF // TF)
         def _(n):
             col = pl.ds(pl.multiple_of(n * TF, TF), TF)
@@ -333,8 +331,7 @@
         r = pl.ds(w * GR, GR)
         return extra(rows.at[1 - d, r], dprows.at[r], pdp)
 
-    def dp_pre(w):
-        r = pl.ds(w * GR, GR)
+    def dp_pre(r):
         return [extra(pre.at[i, r], dppre.at[i, r], pdp) for i in range(2)]
 
     FB = FF // 2
@@ -381,32 +378,33 @@
     sent_first(T1)
     forward_out(1, O1)
     arrived(G0)
-    unpack(G0, put_grads, 0)
-    backward(0)
-    dp_in += dp_pre(0)
+    for dc in range(2):
+        unpack(G0, put_grads, 0, (dc,))
+        backward(pl.ds(dc * CR, CR))
+        dp_in += dp_pre(pl.ds(dc * CR, CR))
     second_legs(G1)
     first_legs(O0)
     sent_first(G0)
     backward_rows(0, R0)
-    first_legs(O1)
     arrived(G1)
     unpack(G1, put_grads, 1)
-    backward(1)
-    dp_in += dp_pre(1)
+    backward(pl.ds(GR, GR))
+    dp_in += dp_pre(pl.ds(GR, GR))
     second_legs(O0)
+    first_legs(O1)
     sent_first(G1)
     backward_rows(1, R1)
-    first_legs(R1)
     for n in range(2):
         wide[:, pl.ds(n * HALF, HALF)] = down_part(n, other).astype(BF)
     dp_down = extra(wide, dpdown, pdp)
     second_legs(O1)
-    first_legs(R0)
+    first_legs(R1)
     for n in range(2):
         own = down_part(n, mine)
         act[n, pl.ds(0, FB), :] = own[:, :FF]
         act[n, pl.ds(FB, FB), pl.ds(0, HALF - FF)] = own[:, FF:]
     second_legs(R1)
+    first_legs(R0)
     own_back = route(own_ids, own_probs, -1)
     z_back = route(z_ids_v, z_probs_v, -1)
     arrived(O1)

time: 163 us -> 163 us (level)
  no operation moved by 1% of the time
where the time goes in v5:
time: 163 us; the launch traced here: 162 us
  Pallas kernels  162 us (99%)
    pallas_call x1, Pallas kernels, per_device(): pl.pallas_call(kernel, out_shape=(V((tok_n, D), BF), V((tok_n, D), BF), V...  159 us

profile of v5, /device:TPU:1, one launch (start us, length us, event | category | flops | bytes accessed | tf_op | source)
XLA Modules:
  0.0 162.5 jit_solution(8405009284545241748)
XLA Ops:
  0.6 159.1 %moe.1 = (bf16[128,2048]{1,0:T(8,128)(2,1)S(1)}, bf16[128,2048]{1,0:T(8,128)(2,1)S(1)}, f32[4,128]{1,0:T(4,128)S(1)}, bf16[1024,768]{1,0:T(8,128)(2,1)S(1)}, bf1...) custom-call(s32[4,128]{1,0:T(4,128)} %bitcast.15, ...), custom_call_target="tpu_custom_call" | custom-call | flops 21743271936 | bytes 20971520 | tf_op jit(solution)/shard_map/moe/pallas_call | solution.py:499
  159.7 2.6 %hand_over.1 = (bf16[128,2048]{1,0:T(8,128)(2,1)}, bf16[128,2048]{1,0:T(8,128)(2,1)}, f32[4,128]{1,0:T(4,128)}, bf16[1024,768]{1,0:T(8,128)(2,1)}, bf16[1024,768]{1,0:T(8,128)(2,1)}, /*index=5*/bf16[768,1024]{1,0:T(8,128)(2,1)}) custom-call(bf16[128,2048]{1,0:T(8,128)(2,1)S(1)} %get-tuple-element.18.refs_0_, ...), custom_call_target="tpu_custom_call" | custom-call | tf_op jit(solution)/shard_map/hand_over/pallas_call | solution.py:531
